TPU v7x, 256 devices: a whole 4x4x8 slice. The times are simulated.
256 devices in a mesh: row: 16 (over z, core), col: 16 (over y, x).
Axes of the slice: x: 4, y: 4, z: 8, core: 2. Of those that a mesh axis runs over, the one named last changes fastest.
Arguments:
- object_slices: float32 [2, 2, 4096, 4096], P(None, None, 'row', 'col'), may hold values from -5 to 5
- probe_wave: float32 [2, 256, 256], replicated, may hold values from -6 to 6
- propagator: float32 [2, 256, 256], replicated, may hold values from -5 to 5
- measured: float32 [16, 16, 4, 256, 256], P('row', 'col'), as said below
- positions: int32 [16, 16, 4, 2], P('row', 'col'), may hold values from -128 to 128, as said below
- scan_counts: int32 [16, 16], P('row', 'col'), may hold values from 1 to 4, as said below
Outputs:
- object_grad: float32 [2, 2, 4096, 4096], P(None, None, 'row', 'col')
- probe_grad: float32 [2, 256, 256], replicated
Inputs may be any that keep to these rules, and one draw needn't show every extreme that they name: `positions`: every patch of 256 x 256 cells lies inside the object window. Slots k < scan_counts[r, c] of tile (r, c) are used, the others are ignored. `measured`: positive intensities.
All inputs are finite; a program needn't handle non-finite values.
Results may differ from a plain program's by a relative error of at most 0.0003.
Values sent between devices are 32-bit elements; how exact they have to be, the bound alone decides.
A program may use at most 128 MiB of HBM per device.

v0:
```python
import math

import jax
import jax.numpy as jnp
from jax import lax
from jax.sharding import PartitionSpec as P

precision_mode = lax.Precision.HIGHEST


def padded(cells, sides, width):
    for axis, dim in sides:
        count = lax.axis_size(axis)
        ends = count - 1
        head = lax.slice_in_dim(cells, 0, width, axis=dim)
        tail = lax.slice_in_dim(cells, cells.shape[dim] - width, cells.shape[dim], axis=dim)
        cells = jnp.concatenate(
            [
                lax.ppermute(tail, axis, [(i, (i + 1) % count) for i in range(ends)]),
                cells,
                lax.ppermute(head, axis, [((i + 1) % count, i) for i in range(ends)]),
            ],
            axis=dim,
        )
    return cells


def dft_tables(width):
    indices = jnp.arange(width, dtype=jnp.int32)
    phases = indices[:, None] * indices[None, :] % width
    angles = phases.astype(jnp.float32) * (2.0 * math.pi / width)
    factor = 1.0 / math.sqrt(width)
    return (jnp.cos(angles) * factor, jnp.sin(angles) * factor)


def matrix_dot(first, second):
    return jnp.dot(first, second, precision=precision_mode, preferred_element_type=jnp.float32)


def complex_dot(first, second):
    real_part = matrix_dot(first[0], second[0]) - matrix_dot(first[1], second[1])
    imag_part = matrix_dot(first[0], second[1]) + matrix_dot(first[1], second[0])
    return (real_part, imag_part)


def fourier(field, tables, direction):
    matrix = (tables[0], direction * tables[1])
    return complex_dot(complex_dot(matrix, field), matrix)


def complex_mul(first, second):
    return (
        first[0] * second[0] - first[1] * second[1],
        first[0] * second[1] + first[1] * second[0],
    )


def conj_mul(first, second):
    return (
        first[0] * second[0] + first[1] * second[1],
        first[0] * second[1] - first[1] * second[0],
    )


def slot_gradient(patch, probe_wave, propagator, target, tables):
    layers = patch.shape[0]
    kernel = (propagator[0], propagator[1])
    wave = (probe_wave[0], probe_wave[1])
    incoming = []
    for layer_at in range(layers):
        incoming.append(wave)
        exited = complex_mul(wave, (patch[layer_at, 0], patch[layer_at, 1]))
        if layer_at + 1 < layers:
            wave = fourier(complex_mul(kernel, fourier(exited, tables, -1.0)), tables, 1.0)
    far_field = fourier(exited, tables, -1.0)
    misfit = far_field[0] * far_field[0] + far_field[1] * far_field[1] - target
    adjoint = fourier((misfit * far_field[0], misfit * far_field[1]), tables, 1.0)
    gradients = [None] * layers
    for layer_at in range(layers - 1, -1, -1):
        gradients[layer_at] = jnp.stack(conj_mul(incoming[layer_at], adjoint))
        adjoint = conj_mul((patch[layer_at, 0], patch[layer_at, 1]), adjoint)
        if layer_at > 0:
            adjoint = fourier(conj_mul(kernel, fourier(adjoint, tables, -1.0)), tables, 1.0)
    return (jnp.stack(gradients), jnp.stack(adjoint))


def add_block(base, block, row_start, col_start):
    return base.at[
        :, :, row_start : row_start + block.shape[2], col_start : col_start + block.shape[3]
    ].add(block)


def on_device(object_slices, probe_wave, propagator, measured, positions, scan_counts):
    layers = object_slices.shape[0]
    tile = object_slices.shape[2]
    width = probe_wave.shape[1]
    half = width // 2
    slots = measured.shape[2]
    tables = dft_tables(width)
    extended = padded(object_slices, (("row", 2), ("col", 3)), half)
    count = scan_counts[0, 0]
    valid = (jnp.arange(slots, dtype=jnp.int32) < count).astype(jnp.float32)
    local_total = jnp.sum(valid * jnp.sum(measured[0, 0], axis=(1, 2)))
    local_count = count.astype(jnp.float32)
    total, scans = lax.psum((local_total, local_count), ("row", "col"))

    def slot_starts(slot_at):
        offset = lax.dynamic_index_in_dim(positions[0, 0], slot_at, 0, keepdims=False)
        return (jnp.int32(0), jnp.int32(0), offset[0] + half, offset[1] + half)

    def visit(slot_at, state_pair):
        grad_ext, probe_sum = state_pair
        starts = slot_starts(slot_at)
        patch = lax.dynamic_slice(extended, starts, (layers, 2, width, width))
        target = lax.dynamic_index_in_dim(measured[0, 0], slot_at, 0, keepdims=False)
        gradients, adjoint = slot_gradient(patch, probe_wave, propagator, target, tables)
        region = lax.dynamic_slice(grad_ext, starts, (layers, 2, width, width)) + gradients
        grad_ext = lax.dynamic_update_slice(grad_ext, region, starts)
        return (grad_ext, probe_sum + adjoint)

    initial = (jnp.zeros_like(extended), jnp.zeros((2, width, width), jnp.float32))
    grad_ext, probe_sum = lax.fori_loop(0, count, visit, initial)
    edge_far = tile + half
    strips = jnp.concatenate((grad_ext[:, :, :half, :], grad_ext[:, :, edge_far:, :]), axis=2)
    rows_in = padded(strips, (("row", 2),), half)
    middle = grad_ext[:, :, half:edge_far, :]
    middle = add_block(middle, rows_in[:, :, :half, :], 0, 0)
    middle = add_block(middle, rows_in[:, :, 3 * half :, :], tile - half, 0)
    strips = jnp.concatenate((middle[:, :, :, :half], middle[:, :, :, edge_far:]), axis=3)
    cols_in = padded(strips, (("col", 3),), half)
    owned = middle[:, :, :, half:edge_far]
    owned = add_block(owned, cols_in[:, :, :, :half], 0, 0)
    owned = add_block(owned, cols_in[:, :, :, 3 * half :], 0, tile - half)
    probe_all = lax.psum(probe_sum, ("row", "col"))
    mean_level = total / (scans * (width * width))
    return (owned / mean_level, probe_all / (mean_level * scans))


def solution(mesh):
    placed = (
        P(None, None, "row", "col"),
        P(),
        P(),
        P("row", "col", None, None, None),
        P("row", "col", None, None),
        P("row", "col"),
    )
    return jax.shard_map(
        on_device,
        mesh=mesh,
        in_specs=placed,
        out_specs=(P(None, None, "row", "col"), P()),
        check_vma=False,
    )
```

profile of v0, /device:TPU:1, one launch (start us, length us, event | category | flops | bytes accessed | tf_op | source)
XLA Modules:
  0.0 759.9 jit_solution(12097574579112852666)
XLA Ops:
  8.6 4.9 collective-permute-start
  13.5 1.9 collective-permute-start.1
  15.4 4.2 collective-permute-done
  19.8 4.3 collective-permute-done.1
  25.2 4.5 collective-permute-start.2
  31.0 14.4 %collective-permute-done.2 = f32[2,2,512,128]{3,2,1,0:T(8,128)} collective-permute-done((f32[2,2,512,128]{3,2,1,0:T(8,128)}, f32[2,2,512,128]{3,2,1,0:T(8,128)}, u32[]{:S(2)}, u32[]{:S(2)}) %collective-permute-start.2) | collective-permute-done | bytes 1048608 | tf_op jit(solution)/shard_map/ppermute | solution.py:19
  45.3 4.9 collective-permute-done.3
  50.2 3.9 pad_maximum_fusion
  54.2 2.5 broadcast_in_dim.8
  56.8 294.4 %while.21 = (s32[]{:T(128)}, f32[2,2,512,512]{3,2,1,0:T(8,128)}, f32[2,256,256]{2,1,0:T(8,128)S(1)}, s32[]{:T(128)}, s32[1,1,4,2]{2,3,1,0:T(2,128)S(1)}, /*index...) while((s32[]{:T(128)}, f32[2,2,512,512]{3,2,1,0:T(8,128)}, ...), condition=%wide.region_1.2_spmd.clone.clone, body=%wide.region_0.1_spmd.clone.clone.sunk | while | flops 9717022720 | bytes 50332104 | solution.py:122
  63.5 1.5 convolution_add_fusion.22
  66.5 1.5 convolution_subtract_fusion.20
  72.4 3.1 fusion.449
  86.0 2.8 multiply_add_fusion.3
  90.3 1.5 convolution_add_fusion.25
  93.2 1.5 convolution_subtract_fusion.23
  99.2 1.7 fusion.456
  111.2 3.1 multiply_subtract_fusion.3
  115.9 1.5 convolution_add_fusion.28
  118.8 1.5 convolution_subtract_fusion.26
  124.8 2.7 fusion.463
  137.8 2.7 add_bitcast_fusion.3
  140.7 1.8 maximum_add_fusion.4
  142.6 9.1 %dynamic_update_slice.10 = f32[2,2,512,512]{3,2,1,0:T(8,128)} dynamic-update-slice(f32[2,2,512,512]{3,2,1,0:T(8,128)} %get-tuple-element.631, f32[2,2,256,256]{3,2,1,0:T(8,128)S(1)} %maximum_add_fusion.4, s32[]{:T(128)} %constant.177.clone.1..sunk, s32[]{:T(128)} %constant.177.clone.1..sunk, s32[]{:T(128)S(6)} %select_n.317, s32[]{:T(128)S(6)} %select_n.318) | dynamic-update-slice | bytes 2097156 | tf_op jit(solution)/shard_map/while/body/dynamic_update_slice | solution.py:118
  158.5 1.5 convolution_add_fusion.22
  161.5 1.5 convolution_subtract_fusion.20
  167.5 2.7 fusion.449
  180.6 2.9 multiply_add_fusion.3
  184.9 1.5 convolution_add_fusion.25
  187.9 1.5 convolution_subtract_fusion.23
  190.9 1.5 convolution_subtract_fusion.24
  193.9 1.9 fusion.456
  206.1 2.9 multiply_subtract_fusion.3
  210.4 1.5 convolution_add_fusion.28
  213.4 1.5 convolution_subtract_fusion.26
  219.4 2.9 fusion.463
  232.6 2.7 add_bitcast_fusion.3
  235.6 1.8 maximum_add_fusion.4
  237.4 11.8 %dynamic_update_slice.10 = f32[2,2,512,512]{3,2,1,0:T(8,128)} dynamic-update-slice(f32[2,2,512,512]{3,2,1,0:T(8,128)} %get-tuple-element.631, f32[2,2,256,256]{3,2,1,0:T(8,128)S(1)} %maximum_add_fusion.4, s32[]{:T(128)} %constant.177.clone.1..sunk, s32[]{:T(128)} %constant.177.clone.1..sunk, s32[]{:T(128)S(6)} %select_n.317, s32[]{:T(128)S(6)} %select_n.318) | dynamic-update-slice | bytes 2097156 | tf_op jit(solution)/shard_map/while/body/dynamic_update_slice | solution.py:118
  255.8 1.5 convolution_add_fusion.22
  258.8 1.5 convolution_subtract_fusion.20
  264.8 2.8 fusion.449
  277.9 3.1 multiply_add_fusion.3
  282.5 1.5 convolution_add_fusion.25
  285.4 1.5 convolution_subtract_fusion.23
  288.4 1.5 convolution_subtract_fusion.24
  291.4 1.7 fusion.456
  303.4 3.1 multiply_subtract_fusion.3
  308.0 1.5 convolution_add_fusion.28
  311.0 1.5 convolution_subtract_fusion.26
  316.9 2.7 fusion.463
  330.0 2.7 add_bitcast_fusion.3
  332.9 1.8 maximum_add_fusion.4
  334.7 11.8 %dynamic_update_slice.10 = f32[2,2,512,512]{3,2,1,0:T(8,128)} dynamic-update-slice(f32[2,2,512,512]{3,2,1,0:T(8,128)} %get-tuple-element.631, f32[2,2,256,256]{3,2,1,0:T(8,128)S(1)} %maximum_add_fusion.4, s32[]{:T(128)} %constant.177.clone.1..sunk, s32[]{:T(128)} %constant.177.clone.1..sunk, s32[]{:T(128)S(6)} %select_n.317, s32[]{:T(128)S(6)} %select_n.318) | dynamic-update-slice | bytes 2097156 | tf_op jit(solution)/shard_map/while/body/dynamic_update_slice | solution.py:118
  351.2 1.5 slice.230
  352.7 8.9 %collective-permute-start.4 = (f32[2,2,128,512]{3,2,1,0:T(8,128)S(1)}, f32[2,2,128,512]{3,2,1,0:T(8,128)S(1)}, u32[]{:S(2)}, u32[]{:S(2)}) collective-permute-start(f32[2,2,128,512]{3,2,1,0:T(8,128)S(1)} %slice.230), channel_id=1, source_target_pairs={{0,16},{16,32},{32,48},{48,64},{64,80},{80,96},{96,112},{112,128},... | collective-permute-start | bytes 3145736 | tf_op jit(solution)/shard_map/ppermute | solution.py:19
  361.6 1.8 slice.228
  363.4 9.9 %collective-permute-done.4 = f32[2,2,128,512]{3,2,1,0:T(8,128)S(1)} collective-permute-done((f32[2,2,128,512]{3,2,1,0:T(8,128)S(1)}, f32[2,2,128,512]{3,2,1,0:T(8,128)S(1)}, u32[]{:S(2)}, u32[]{:S(2)}) %collective-permute-start.4) | collective-permute-done | bytes 1048608 | tf_op jit(solution)/shard_map/ppermute | solution.py:19
  373.7 1.9 collective-permute-start.5
  375.6 15.2 %collective-permute-done.5 = f32[2,2,128,512]{3,2,1,0:T(8,128)S(1)} collective-permute-done((f32[2,2,128,512]{3,2,1,0:T(8,128)S(1)}, f32[2,2,128,512]{3,2,1,0:T(8,128)S(1)}, u32[]{:S(2)}, u32[]{:S(2)}) %collective-permute-start.5) | collective-permute-done | bytes 1048608 | tf_op jit(solution)/shard_map/ppermute | solution.py:21
  393.5 2.2 collective-permute-start.6
  398.5 183.7 %all-reduce = (f32[]{:T(128)}, f32[]{:T(128)}) all-reduce(f32[]{:T(128)} %fusion.272, f32[]{:T(128)S(6)} %convert_element_type.102), channel_id=1, replica_groups=mesh['row'=16,'col'=16] {'row','col'}, use_global_device_ids=true, to_apply=%region_4.5 | all-reduce | flops 2 | bytes 16 | tf_op jit(solution)/shard_map/psum | solution.py:105
  584.1 164.4 %all-reduce.3.cloned.1.call-done = f32[2,256,256]{2,1,0:T(8,128)} async-done(((f32[2,256,256]{2,1,0:T(8,128)}), f32[2,256,256]{2,1,0:T(8,128)}) %all-reduce.3.cloned.1.call-update) | async-done | bytes 524304 | tf_op jit(solution)/shard_map/psum | solution.py:134
  748.5 1.9 broadcast_divide_fusion.1
  (158 shorter events, 173.9 us)
Async XLA Ops:
  7.2 12.5 %copy-start.5 = (f32[2,2,256,256]{3,2,1,0:T(8,128)S(1)}, f32[2,2,256,256]{3,2,1,0:T(8,128)}, u32[]{:S(2)}) copy-start(f32[2,2,256,256]{3,2,1,0:T(8,128)} %param.16) | copy-start | bytes 3145732
  7.2 741.3 %all-reduce.3.cloned.1.call-start = ((), (), s32[]{:S(2)}) async-start(), calls=%async_computation | async-start | bytes 1048576 | tf_op jit(solution)/shard_map/psum | solution.py:134
  8.6 11.0 %collective-permute-start = (f32[2,2,128,256]{3,2,1,0:T(8,128)S(1)}, f32[2,2,128,256]{3,2,1,0:T(8,128)S(1)}, u32[]{:S(2)}, u32[]{:S(2)}) collective-permute-start(f32[2,2,128,256]{3,2,1,0:T(8,128)S(1)} %get-tuple-element.510), channel_id=1, source_target_pairs={{0,16},{16,32},{32,48},{48,64},{64,80},{80,96},{96,112},{112,128},... | collective-permute-start | bytes 1572872 | tf_op jit(solution)/shard_map/ppermute | solution.py:19
  13.5 10.5 %collective-permute-start.1 = (f32[2,2,128,256]{3,2,1,0:T(8,128)S(1)}, f32[2,2,128,256]{3,2,1,0:T(8,128)S(1)}, u32[]{:S(2)}, u32[]{:S(2)}) collective-permute-start(f32[2,2,128,256]{3,2,1,0:T(8,128)S(1)} %get-tuple-element.509), channel_id=1, source_target_pairs={{16,0},{32,16},{48,32},{64,48},{80,64},{96,80},{112,96},{128,112},... | collective-permute-start | bytes 1572872 | tf_op jit(solution)/shard_map/ppermute | solution.py:21
  25.2 20.2 %collective-permute-start.2 = (f32[2,2,512,128]{3,2,1,0:T(8,128)}, f32[2,2,512,128]{3,2,1,0:T(8,128)}, u32[]{:S(2)}, u32[]{:S(2)}) collective-permute-start(f32[2,2,512,128]{3,2,1,0:T(8,128)} %get-tuple-element.507), channel_id=1, source_target_pairs={{0,1},{1,2},{2,3},{3,4},{4,5},{5,6},{6,7},{7,8},{8,9},{9,10},{10,1... | collective-permute-start | bytes 3145736 | tf_op jit(solution)/shard_map/ppermute | solution.py:19
  29.7 20.5 %collective-permute-start.3 = (f32[2,2,512,128]{3,2,1,0:T(8,128)S(1)}, f32[2,2,512,128]{3,2,1,0:T(8,128)}, u32[]{:S(2)}, u32[]{:S(2)}) collective-permute-start(f32[2,2,512,128]{3,2,1,0:T(8,128)S(1)} %get-tuple-element.508), channel_id=1, source_target_pairs={{1,0},{2,1},{3,2},{4,3},{5,4},{6,5},{7,6},{8,7},{9,8},{10,9},{11,1... | collective-permute-start | bytes 3145736 | tf_op jit(solution)/shard_map/ppermute | solution.py:21
  54.1 2.6 copy-start.1
  54.2 2.6 copy-start.6
  54.2 2.6 copy-start.7
  351.1 12.2 %copy-start.2 = (f32[2,256,256]{2,1,0:T(8,128)}, f32[2,256,256]{2,1,0:T(8,128)S(1)}, u32[]{:S(2)}) copy-start(f32[2,256,256]{2,1,0:T(8,128)S(1)} %get-tuple-element.359) | copy-start | bytes 1572868
  352.7 20.7 %copy-start = (f32[2,2,512,512]{3,2,1,0:T(8,128)S(1)}, f32[2,2,512,512]{3,2,1,0:T(8,128)}, u32[]{:S(2)}) copy-start(f32[2,2,512,512]{3,2,1,0:T(8,128)} %get-tuple-element.358) | copy-start | bytes 12582916
  352.7 20.6 %collective-permute-start.4 = (f32[2,2,128,512]{3,2,1,0:T(8,128)S(1)}, f32[2,2,128,512]{3,2,1,0:T(8,128)S(1)}, u32[]{:S(2)}, u32[]{:S(2)}) collective-permute-start(f32[2,2,128,512]{3,2,1,0:T(8,128)S(1)} %slice.230), channel_id=1, source_target_pairs={{0,16},{16,32},{32,48},{48,64},{64,80},{80,96},{96,112},{112,128},... | collective-permute-start | bytes 3145736 | tf_op jit(solution)/shard_map/ppermute | solution.py:19
  373.7 17.2 %collective-permute-start.5 = (f32[2,2,128,512]{3,2,1,0:T(8,128)S(1)}, f32[2,2,128,512]{3,2,1,0:T(8,128)S(1)}, u32[]{:S(2)}, u32[]{:S(2)}) collective-permute-start(f32[2,2,128,512]{3,2,1,0:T(8,128)S(1)} %get-tuple-element.503), channel_id=1, source_target_pairs={{16,0},{32,16},{48,32},{64,48},{80,64},{96,80},{112,96},{128,112},... | collective-permute-start | bytes 3145736 | tf_op jit(solution)/shard_map/ppermute | solution.py:21
  391.1 1.3 copy-start.3
  393.5 356.9 %copy-start.4 = (f32[2,2,256,512]{3,2,1,0:T(8,128)S(1)}, f32[2,2,256,512]{3,2,1,0:T(8,128)}, u32[]{:S(2)}) copy-start(f32[2,2,256,512]{3,2,1,0:T(8,128)} %copy-done.3) | copy-start | bytes 6291460
  393.5 357.0 %collective-permute-start.6 = (f32[2,2,256,128]{3,2,1,0:T(8,128)}, f32[2,2,256,128]{3,2,1,0:T(8,128)}, u32[]{:S(2)}, u32[]{:S(2)}) collective-permute-start(f32[2,2,256,128]{3,2,1,0:T(8,128)} %get-tuple-element.506), channel_id=1, source_target_pairs={{0,1},{1,2},{2,3},{3,4},{4,5},{5,6},{6,7},{7,8},{8,9},{9,10},{10,1... | collective-permute-start | bytes 1572872 | tf_op jit(solution)/shard_map/ppermute | solution.py:19
  396.6 355.0 %collective-permute-start.7 = (f32[2,2,256,128]{3,2,1,0:T(8,128)}, f32[2,2,256,128]{3,2,1,0:T(8,128)S(1)}, u32[]{:S(2)}, u32[]{:S(2)}) collective-permute-start(f32[2,2,256,128]{3,2,1,0:T(8,128)} %get-tuple-element.505), channel_id=1, source_target_pairs={{1,0},{2,1},{3,2},{4,3},{5,4},{6,5},{7,6},{8,7},{9,8},{10,9},{11,1... | collective-permute-start | bytes 1572872 | tf_op jit(solution)/shard_map/ppermute | solution.py:21
Sparse Core Ops, SparseCore 0:
  395.9 352.5 all-reduce.2
where the time goes:
time: 765 us; the launch traced here: 760 us
  matrix products  234 us (31%)
  waiting for transfers between devices  217 us (28%)
  blocking collectives  184 us (24%)
  local copies, waits for them, and re-layouts  45.4 us (6%)
  starting transfers between devices  27 us (4%)
  other arithmetic  19.7 us (3%)
  between operations  17 us (2%)
  loops' own time  15.9 us (2%)
    dot_general x144, matrix products, matrix_dot(): jnp.dot(first, second, precision=precision_mode, preferred_element_type=j...  234 us
    psum x1, blocking collectives, on_device(): total, scans = lax.psum((local_total, local_count), ('row', 'col'))  184 us
    psum x1, waiting for transfers between devices, on_device(): probe_all = lax.psum(probe_sum, ('row', 'col'))  164 us
    dynamic_update_slice x3, local copies, waits for them, and re-layouts, visit(): grad_ext = lax.dynamic_update_slice(grad_ext, region, starts)  32.7 us
    ppermute x4, waiting for transfers between devices, padded(): lax.ppermute(tail, axis, [(i, (i + 1) % count) for i in range(ends)])  28.5 us
    ppermute x4, waiting for transfers between devices, padded(): lax.ppermute(head, axis, [((i + 1) % count, i) for i in range(ends)])  24.4 us
    ppermute x4, starting transfers between devices, padded(): lax.ppermute(tail, axis, [(i, (i + 1) % count) for i in range(ends)])  20.6 us
    another operation x1, loops' own time, on_device(): grad_ext, probe_sum = lax.fori_loop(0, count, visit, initial)  15.9 us
  transfers between devices with their start and end apart: 9, of which 7 were waited for; matrix products, arithmetic and copies ran while one was open for 1% of the time, Pallas kernels for 0%

commit v1 on v0

v1 whole, which is shorter than its diff:
```python
import functools
import math

import jax
import jax.numpy as jnp
import ml_dtypes
import numpy as np
from jax import lax
from jax.experimental import pallas as pl
from jax.experimental.pallas import tpu as pltpu
from jax.sharding import PartitionSpec as P

F32, BF16 = jnp.float32, jnp.bfloat16
MESH = pl.DeviceIdType.MESH
EVEN, EVEN_T, ODD, ODD_T = 0, 2, 4, 6
CHUNK = 32


def split_table(table):
    high = table.astype(ml_dtypes.bfloat16)
    return [high, (table - high.astype(np.float64)).astype(ml_dtypes.bfloat16)]


def dft_tables(width):
    half = width // 2
    out = []
    for parity in range(2):
        k = np.arange(half)[:, None] * 2 + parity
        n = np.arange(half)[None, :]
        angle = 2.0 * math.pi * ((k * n) % width) / width
        c, s = np.cos(angle) / math.sqrt(width), np.sin(angle) / math.sqrt(width)
        block = np.block([[c, s], [-s, c]])
        out += split_table(block) + split_table(block.T)
    return np.stack(out)


def order_tables(width):
    half = width // 2
    order = np.concatenate([np.arange(half) * 2, np.arange(half) * 2 + 1])
    perm = np.zeros((width, width))
    perm[order, np.arange(width)] = 1.0
    return np.stack([perm, perm.T]).astype(ml_dtypes.bfloat16)


def cat(parts, axis):
    return jnp.concatenate(parts, axis=axis)


def split(x):
    high = x.astype(BF16)
    return high, (x - high.astype(F32)).astype(BF16)


def mm(a, b):
    return jnp.dot(a, b, preferred_element_type=F32)


def right(x, tables, at):
    high, low = split(x)
    th, tl = tables[at], tables[at + 1]
    return mm(high, th) + mm(low, th) + mm(high, tl)


def left(tables, at, x):
    high, low = split(x)
    th, tl = tables[at], tables[at + 1]
    return mm(th, high) + mm(th, low) + mm(tl, high)


def forward(re, im, tables):
    h = re.shape[1] // 2
    u = cat([re[:, :h] + re[:, h:], im[:, :h] + im[:, h:]], 1)
    v = cat([re[:, :h] - re[:, h:], im[:, :h] - im[:, h:]], 1)
    e, o = right(u, tables, EVEN_T), right(v, tables, ODD_T)
    es, os = e[:h] + e[h:], o[:h] + o[h:]
    ed, od = e[:h] - e[h:], o[:h] - o[h:]
    a = cat([cat([es[:, :h], os[:, :h]], 1), cat([es[:, h:], os[:, h:]], 1)], 0)
    b = cat([cat([ed[:, :h], od[:, :h]], 1), cat([ed[:, h:], od[:, h:]], 1)], 0)
    return left(tables, EVEN, a), left(tables, ODD, b)


def inverse(a, b, tables):
    h = a.shape[0] // 2
    e, o = left(tables, EVEN_T, a), left(tables, ODD_T, b)
    t, w = e + o, e - o
    qe = cat([cat([t[:h, :h], t[h:, :h]], 1), cat([w[:h, :h], w[h:, :h]], 1)], 0)
    qo = cat([cat([t[:h, h:], t[h:, h:]], 1), cat([w[:h, h:], w[h:, h:]], 1)], 0)
    e, o = right(qe, tables, EVEN), right(qo, tables, ODD)
    s, d = e + o, e - o
    return cat([s[:, :h], d[:, :h]], 1), cat([s[:, h:], d[:, h:]], 1)


def freq_mul(a, k, conj):
    h = a.shape[0] // 2
    kr, ki, ar, ai = k[:h], k[h:], a[:h], a[h:]
    if conj:
        return cat([kr * ar + ki * ai, kr * ai - ki * ar], 0)
    return cat([kr * ar - ki * ai, kr * ai + ki * ar], 0)


def reorder(x, order):
    high, low = split(x)
    high, low = split(mm(high, order[0]) + mm(low, order[0]))
    return mm(order[1], high) + mm(order[1], low)


def turn(x, down, along):
    return pltpu.roll(pltpu.roll(x, along, 1), down, 0)


def kernel(
    W, NR, NC,
    obj, probe, prop, meas, pos, cnt, tables, order,
    grad_out, probe_out,
    ext, gext, kperm, mperm, probes, waves, grads, psum,
    rbuf, cbuf, pieces, landed, tiles, tile_landed, tile_all, piece_all,
    own_sem, halo_send, halo_recv, grow_send, grow_recv, gcol_send, gcol_recv,
    rs_send, rs_recv, rt_send, rt_recv, ag_send, ag_recv, ac_send, ac_recv,
):
    h = W // 2
    cap = meas.shape[0]
    row, col = lax.axis_index("row"), lax.axis_index("col")
    up, down = lax.rem(row + NR - 1, NR), lax.rem(row + 1, NR)
    lft, rgt = lax.rem(col + NC - 1, NC), lax.rem(col + 1, NC)
    to_up, to_down, to_left, to_right = (up, col), (down, col), (row, lft), (row, rgt)
    piece_rows = 4 * W // NC
    zs = NR // 2
    tile_rows = piece_rows // zs

    def remote(src, dst, send, recv, device):
        return pltpu.make_async_remote_copy(
            src_ref=src, dst_ref=dst, send_sem=send, recv_sem=recv,
            device_id=device, device_id_type=MESH,
        )

    barrier = pltpu.get_barrier_semaphore()

    def greet_col(d, carry):
        pl.semaphore_signal(barrier, inc=1, device_id=(row, lax.rem(col + d, NC)), device_id_type=MESH)
        return carry

    def greet_row(d, carry):
        pl.semaphore_signal(barrier, inc=1, device_id=(lax.rem(row + d, NR), col), device_id_type=MESH)
        return carry

    lax.fori_loop(1, NC, greet_col, 0)
    lax.fori_loop(1, NR, greet_row, 0)
    own = pltpu.make_async_copy(obj, ext.at[:, :, h:h + W, h:h + W], own_sem)
    own.start()
    pl.semaphore_wait(barrier, NC + NR - 2)

    far = h + W
    halos = []
    for s in range(2):
        sides = []
        for q in range(2):
            here = pl.ds(q * h, h)
            there = pl.ds(h + q * h, h)
            for side in range(2):
                n = s * 10 + q * 2 + side
                src = obj.at[s, :, here, pl.ds(h, h)] if side == 0 else obj.at[s, :, here, pl.ds(0, h)]
                dst = ext.at[s, :, there, pl.ds(0, h)] if side == 0 else ext.at[s, :, there, pl.ds(far, h)]
                sides.append(remote(src, dst, halo_send.at[n], halo_recv.at[n], to_right if side == 0 else to_left))
        middles = [
            remote(obj.at[s, :, pl.ds(0, h), :], ext.at[s, :, pl.ds(far, h), pl.ds(h, W)],
                   halo_send.at[s * 10 + 4], halo_recv.at[s * 10 + 4], to_up),
            remote(obj.at[s, :, pl.ds(h, h), :], ext.at[s, :, pl.ds(0, h), pl.ds(h, W)],
                   halo_send.at[s * 10 + 5], halo_recv.at[s * 10 + 5], to_down),
        ]
        corners = []
        for q in range(2):
            for side in range(2):
                n = s * 10 + 6 + q * 2 + side
                lanes = pl.ds(0, h) if side == 0 else pl.ds(far, h)
                corners.append(remote(
                    ext.at[s, :, pl.ds(h + q * h, h), lanes],
                    ext.at[s, :, pl.ds(far, h) if q == 0 else pl.ds(0, h), lanes],
                    halo_send.at[n], halo_recv.at[n], to_up if q == 0 else to_down,
                ))
        halos.append((sides, middles, corners))
    for sides, middles, corners in halos:
        for c in sides + middles:
            c.start()

    def forward_corners(s):
        sides, middles, corners = halos[s]
        for side, corner in zip(sides, corners):
            side.wait_recv()
            corner.start()

    def finish_halo(s):
        sides, middles, corners = halos[s]
        for c in middles + corners:
            c.wait_recv()

    rows = lax.broadcasted_iota(jnp.int32, (W, W), 0)
    cols = lax.broadcasted_iota(jnp.int32, (W, W), 1)
    count = cnt[0]
    starts = [
        (jnp.clip(pos[2 * k] + h, 0, W), jnp.clip(pos[2 * k + 1] + h, 0, W)) for k in range(cap)
    ]
    kr, ki = reorder(prop[0], order), reorder(prop[1], order)
    kperm[0] = cat([kr[:h], ki[:h]], 0)
    kperm[1] = cat([kr[h:], ki[h:]], 0)

    def start_of(k):
        return jnp.clip(pos[2 * k] + h, 0, W), jnp.clip(pos[2 * k + 1] + h, 0, W)

    def prepare(k, total):
        r0, c0 = start_of(k)
        m = meas[k]
        mperm[k] = reorder(m, order)
        probes[k, 0] = turn(probe[0], lax.rem(r0, W), lax.rem(c0, W))
        probes[k, 1] = turn(probe[1], lax.rem(r0, W), lax.rem(c0, W))
        return total + jnp.where(k < count, jnp.sum(m.reshape(W // 8, 8, W), axis=0), 0.0)

    total = jnp.sum(lax.fori_loop(0, cap, prepare, jnp.zeros((8, W), F32)))
    first_rows = lax.broadcasted_iota(jnp.int32, (8, h), 0) < 4
    level = jnp.where(first_rows, total, count.astype(F32))

    def pick(k, s, ri):
        r0, c0 = start_of(k)
        inr, inc = rows < r0, cols < c0
        q = [[ext[s, ri, a * W:(a + 1) * W, b * W:(b + 1) * W] for b in range(2)] for a in range(2)]
        return jnp.where(inr, jnp.where(inc, q[1][1], q[1][0]), jnp.where(inc, q[0][1], q[0][0]))

    def phase_a(k, carry):
        pr, pi = probes[k, 0], probes[k, 1]
        ore, oim = pick(k, 0, 0), pick(k, 0, 1)
        a, b = forward(pr * ore - pi * oim, pr * oim + pi * ore, tables)
        wr, wi = inverse(freq_mul(a, kperm[0], False), freq_mul(b, kperm[1], False), tables)
        waves[k, 0] = wr
        waves[k, 1] = wi
        return carry

    def phase_b(k, carry):
        wr, wi = waves[k, 0], waves[k, 1]
        ore, oim = pick(k, 1, 0), pick(k, 1, 1)
        a, b = forward(wr * ore - wi * oim, wr * oim + wi * ore, tables)
        fa = a[:h] * a[:h] + a[h:] * a[h:] - mperm[k, :h, :]
        fb = b[:h] * b[:h] + b[h:] * b[h:] - mperm[k, h:, :]
        gr, gi = inverse(cat([fa * a[:h], fa * a[h:]], 0), cat([fb * b[:h], fb * b[h:]], 0), tables)
        wr, wi = waves[k, 0], waves[k, 1]
        grads[k, 0] = wr * gr + wi * gi
        grads[k, 1] = wr * gi - wi * gr
        ore, oim = pick(k, 1, 0), pick(k, 1, 1)
        waves[k, 0] = ore * gr + oim * gi
        waves[k, 1] = ore * gi - oim * gr
        return carry

    def phase_c(k, carry):
        a, b = forward(waves[k, 0], waves[k, 1], tables)
        gr, gi = inverse(freq_mul(a, kperm[0], True), freq_mul(b, kperm[1], True), tables)
        pr, pi = probes[k, 0], probes[k, 1]
        grads[k, 0] = pr * gr + pi * gi
        grads[k, 1] = pr * gi - pi * gr
        ore, oim = pick(k, 0, 0), pick(k, 0, 1)
        r0, c0 = start_of(k)
        used = k < count
        for i, x in enumerate((ore * gr + oim * gi, ore * gi - oim * gr)):
            x = turn(jnp.where(used, x, 0.0), lax.rem(W - r0, W), lax.rem(W - c0, W))
            psum[2 * i * W:(2 * i + 1) * W, :] += x[:, :h]
            psum[(2 * i + 1) * W:(2 * i + 2) * W, :] += x[:, h:]
        return carry

    def place(s):
        chunk_rows = lax.broadcasted_iota(jnp.int32, (CHUNK, W), 0)
        chunk_cols = lax.broadcasted_iota(jnp.int32, (CHUNK, W), 1)

        def one(at, carry):
            base = pl.multiple_of(at * CHUNK, CHUNK)
            inr = [chunk_rows < r0 - base for r0, c0 in starts]
            inc = [chunk_cols < c0 for r0, c0 in starts]
            used = [k < count for k in range(cap)]
            for ri in range(2):
                g = [jnp.where(used[k], grads[k, ri, pl.ds(base, CHUNK), :], 0.0) for k in range(cap)]
                high = [jnp.where(inr[k], g[k], 0.0) for k in range(cap)]
                for qa in range(2):
                    part = high if qa else [g[k] - high[k] for k in range(cap)]
                    far_side = [jnp.where(inc[k], part[k], 0.0) for k in range(cap)]
                    near_side = [part[k] - far_side[k] for k in range(cap)]
                    at_rows = pl.ds(pl.multiple_of(qa * W + base, CHUNK), CHUNK)
                    gext[s, ri, at_rows, pl.ds(0, W)] = sum(near_side[1:], near_side[0])
                    gext[s, ri, at_rows, pl.ds(W, W)] = sum(far_side[1:], far_side[0])
            return carry

        lax.fori_loop(0, W // CHUNK, one, 0)

    row_copies, col_copies = [], []
    for s in range(2):
        parts = []
        for at, (first, size) in enumerate(((0, h), (far, h), (h, W))):
            for d in range(2):
                n = s * 6 + at * 2 + d
                parts.append(remote(
                    gext.at[s, :, pl.ds(0, h) if d == 0 else pl.ds(far, h), pl.ds(first, size)],
                    rbuf.at[s, d, :, :, pl.ds(first, size)],
                    grow_send.at[n], grow_recv.at[n], to_up if d == 0 else to_down,
                ))
        row_copies.append(parts)
        sides = []
        for d in range(2):
            for side in range(2):
                n = s * 4 + d * 2 + side
                sides.append(remote(
                    gext.at[s, :, pl.ds(W, h) if d == 0 else pl.ds(h, h), pl.ds(0, h) if side == 0 else pl.ds(far, h)],
                    cbuf.at[s, d, side],
                    gcol_send.at[n], gcol_recv.at[n], to_left if side == 0 else to_right,
                ))
        col_copies.append(sides)

    def send_rows(s):
        for c in row_copies[s]:
            c.start()

    def send_cols(s):
        for d in range(2):
            at_rows = pl.ds(W, h) if d == 0 else pl.ds(h, h)
            for side in range(2):
                lanes = pl.ds(0, h) if side == 0 else pl.ds(far, h)
                row_copies[s][side * 2 + d].wait_recv()
                for ri in range(2):
                    gext[s, ri, at_rows, lanes] += rbuf[s, d, ri, :, lanes]
                col_copies[s][d * 2 + side].start()

    def finish_grad(s, mean):
        for d in range(2):
            row_copies[s][4 + d].wait_recv()
            q = 1 - d
            for side in range(2):
                col_copies[s][d * 2 + side].wait_recv()
                c = 1 - side
                lanes = pl.ds(h + c * h, h)
                for ri in range(2):
                    grad_out[s, ri, q * h:(q + 1) * h, c * h:(c + 1) * h] = (
                        gext[s, ri, pl.ds(h + q * h, h), lanes]
                        + rbuf[s, d, ri, :, lanes]
                        + cbuf[s, d, side, ri]
                    ) / mean

    psum[...] = jnp.zeros_like(psum)
    own.wait()
    forward_corners(0)
    finish_halo(0)
    lax.fori_loop(0, cap // 2, phase_a, 0)
    forward_corners(1)
    lax.fori_loop(cap // 2, cap, phase_a, 0)
    finish_halo(1)
    lax.fori_loop(0, cap, phase_b, 0)
    place(1)
    send_rows(1)
    lax.fori_loop(0, cap // 2, phase_c, 0)
    send_cols(1)
    lax.fori_loop(cap // 2, cap, phase_c, 0)
    place(0)
    send_rows(0)

    for j in range(NC):
        pieces[j, :piece_rows, :] = psum[j * piece_rows:(j + 1) * piece_rows, :]
        pieces[j, piece_rows:, :] = level

    def scatter_col(d):
        peer = lax.rem(col + d, NC)
        return remote(pieces.at[peer], landed.at[col], rs_send.at[d], rs_recv.at[d], (row, peer))

    def scatter_row(d):
        peer = lax.rem(row + d, NR)
        return remote(tiles.at[lax.div(peer, 2)], tile_landed.at[row], rt_send.at[d], rt_recv.at[d], (peer, col))

    def gather_row(d):
        z = lax.div(row, 2)
        peer = lax.rem(row + 2 * d, NR)
        return remote(tile_all.at[z], tile_all.at[z], ag_send.at[d], ag_recv.at[d], (peer, col))

    def gather_col(d):
        peer = lax.rem(col + d, NC)
        return remote(piece_all.at[col], piece_all.at[col], ac_send.at[d], ac_recv.at[d], (row, peer))

    def run(make, lo, hi, what):
        def step(d, carry):
            getattr(make(d), what)()
            return carry

        lax.fori_loop(lo, hi, step, 0)

    run(scatter_col, 1, NC, "start")
    landed[col] = pieces[col]
    send_cols(0)
    run(scatter_col, 1, NC, "wait_recv")
    got = landed[0]
    for j in range(1, NC):
        got = got + landed[j]
    for z in range(zs):
        tiles[z, :tile_rows, :] = got[z * tile_rows:(z + 1) * tile_rows]
        tiles[z, tile_rows:, :] = got[piece_rows:]
    run(scatter_row, 1, NR, "start")
    tile_landed[row] = tiles[lax.div(row, 2)]
    run(scatter_row, 1, NR, "wait_recv")
    got = tile_landed[0]
    for j in range(1, NR):
        got = got + tile_landed[j]
    total_all = got[tile_rows:tile_rows + 1, :1]
    scans = got[tile_rows + 4:tile_rows + 5, :1]
    mean = total_all / (scans * float(W * W))
    tile_all[lax.div(row, 2)] = got[:tile_rows] / (mean * scans)
    run(gather_row, 1, zs, "start")
    finish_grad(1, mean)
    run(gather_row, 1, zs, "wait_recv")
    for z in range(zs):
        piece_all[col, z * tile_rows:(z + 1) * tile_rows, :] = tile_all[z]
    run(gather_col, 1, NC, "start")
    finish_grad(0, mean)
    run(gather_col, 1, NC, "wait_recv")
    per_half = NC // 4
    for i in range(2):
        for half in range(2):
            for j in range(per_half):
                probe_out[i, j * piece_rows:(j + 1) * piece_rows, half * h:(half + 1) * h] = (
                    piece_all[(2 * i + half) * per_half + j]
                )
    for sides, middles, corners in halos:
        for c in sides + middles + corners:
            c.wait_send()
    for s in range(2):
        for c in row_copies[s] + col_copies[s]:
            c.wait_send()
    run(scatter_col, 1, NC, "wait_send")
    run(scatter_row, 1, NR, "wait_send")
    run(gather_row, 1, zs, "wait_send")
    run(gather_col, 1, NC, "wait_send")


def on_device(NR, NC, object_slices, probe_wave, propagator, measured, positions, scan_counts):
    W = probe_wave.shape[1]
    h = W // 2
    cap = measured.shape[2]
    zs = NR // 2
    piece_rows = 4 * W // NC
    tile_rows = piece_rows // zs
    vmem, smem = pl.BlockSpec(memory_space=pltpu.VMEM), pl.BlockSpec(memory_space=pltpu.SMEM)
    anywhere = pl.BlockSpec(memory_space=pl.ANY)
    V, D = pltpu.VMEM, pltpu.SemaphoreType.DMA
    return pl.pallas_call(
        functools.partial(kernel, W, NR, NC),
        out_shape=(
            jax.ShapeDtypeStruct((2, 2, W, W), F32),
            jax.ShapeDtypeStruct((2, W, W), F32),
        ),
        in_specs=[anywhere, vmem, vmem, vmem, smem, smem, vmem, vmem],
        out_specs=(vmem, vmem),
        scratch_shapes=[
            V((2, 2, 2 * W, 2 * W), F32),
            V((2, 2, 2 * W, 2 * W), F32),
            V((2, W, W), F32),
            V((cap, W, W), F32),
            V((cap, 2, W, W), F32),
            V((cap, 2, W, W), F32),
            V((cap, 2, W, W), F32),
            V((4 * W, h), F32),
            V((2, 2, 2, h, 2 * W), F32),
            V((2, 2, 2, 2, h, h), F32),
            V((NC, piece_rows + 8, h), F32),
            V((NC, piece_rows + 8, h), F32),
            V((zs, tile_rows + 8, h), F32),
            V((NR, tile_rows + 8, h), F32),
            V((zs, tile_rows, h), F32),
            V((NC, piece_rows, h), F32),
            D, D((20,)), D((20,)), D((12,)), D((12,)), D((8,)), D((8,)),
            D((NC,)), D((NC,)), D((NR,)), D((NR,)), D((zs,)), D((zs,)), D((NC,)), D((NC,)),
        ],
        compiler_params=pltpu.CompilerParams(
            collective_id=0, has_side_effects=True, vmem_limit_bytes=56 * 1024 * 1024
        ),
        name="ptychography",
    )(
        object_slices, probe_wave, propagator, measured[0, 0], positions.reshape(-1),
        scan_counts.reshape(-1), jnp.asarray(dft_tables(W)), jnp.asarray(order_tables(W)),
    )


def solution(mesh):
    placed = (
        P(None, None, "row", "col"),
        P(),
        P(),
        P("row", "col", None, None, None),
        P("row", "col", None, None),
        P("row", "col"),
    )
    return jax.shard_map(
        functools.partial(on_device, mesh.shape["row"], mesh.shape["col"]),
        mesh=mesh,
        in_specs=placed,
        out_specs=(P(None, None, "row", "col"), P()),
        check_vma=False,
    )
```

time: 765 us -> 91.1 us (0.12)
  matrix products: 234 us -> 0 us
  waiting for transfers between devices: 217 us -> 0 us
  blocking collectives: 184 us -> 0 us
  Pallas kernels: 0 us -> 84.2 us
  local copies, waits for them, and re-layouts: 45.4 us -> 4.5 us
  starting transfers between devices: 27 us -> 0 us
  other arithmetic: 19.7 us -> 0 us
  loops' own time: 15.9 us -> 0 us
  between operations: 17 us -> 1.3 us
    dot_general x144 -> x0, matrix products: 234 us -> none  [matrix_dot(): jnp.dot(first, second, precision=precision_mode, preferred_element_type=j...]
    psum x1 -> x0, blocking collectives: 184 us -> none  [on_device(): total, scans = lax.psum((local_total, local_count), ('row', 'col'))]
    psum x1 -> x0, waiting for transfers between devices: 164 us -> none  [on_device(): probe_all = lax.psum(probe_sum, ('row', 'col'))]
    pallas_call x0 -> x1, Pallas kernels: none -> 84.2 us  [on_device(): pl.pallas_call(functools.partial(kernel, W, NR, NC), out_shape=(jax.Shape...]
    ppermute x8 -> x0, waiting for transfers between devices: 52.9 us -> none  [the longest x4 28.5 us: padded(): lax.ppermute(tail, axis, [(i, (i + 1) % count) for i in range(ends)])]
    dynamic_update_slice x3 -> x0, local copies, waits for them, and re-layouts: 32.7 us -> none  [visit(): grad_ext = lax.dynamic_update_slice(grad_ext, region, starts)]
    ppermute x8 -> x0, starting transfers between devices: 27 us -> none  [the longest x4 20.6 us: padded(): lax.ppermute(tail, axis, [(i, (i + 1) % count) for i in range(ends)])]
    another operation x1 -> x0, loops' own time: 15.9 us -> none  [on_device(): grad_ext, probe_sum = lax.fori_loop(0, count, visit, initial)]
  transfers between devices with their start and end apart: 9 -> 0, of which waited for: 7 -> 0; matrix products, arithmetic and copies ran while one was open for 1% -> 0% of each run, Pallas kernels for 0% -> 0%
where the time goes in v1:
time: 91.1 us; the launch traced here: 90 us
  Pallas kernels  84.2 us (92%)
  local copies, waits for them, and re-layouts  4.5 us (5%)
  between operations  1.3 us (1%)
    pallas_call x1, Pallas kernels, on_device(): pl.pallas_call(functools.partial(kernel, W, NR, NC), out_shape=(jax.Shape...  84.2 us
    unnamed x7, local copies, waits for them, and re-layouts  3.9 us

profile of v1, /device:TPU:1, one launch (start us, length us, event | category | flops | bytes accessed | tf_op | source)
XLA Modules:
  0.0 90.0 jit_solution(8346800440398110470)
XLA Ops:
  1.3 0.0 copy-start.1
  1.3 0.7 copy-done.1
  2.0 0.1 copy.11
  2.0 0.6 reshape.10.pos
  2.6 84.2 %ptychography.1 = (f32[2,2,256,256]{3,2,1,0:T(8,128)}, f32[2,256,256]{2,1,0:T(8,128)}) custom-call(f32[2,2,256,256]{3,2,1,0:T(8,128)} %obj.1, f32[2,256,256]{2,1,0:T(8,128)} %probe.1, f32[2,256,256]{2,1,0:T(8,128)} %prop.1, f32[4,256,256]{2,1,0:T(8,128)} %bitcast.3, s32[8]{0:T(128)} %reshape.10.pos, s32[1]{0:T(128)} %bitcast.2.cnt, ...), custom_call_target="tpu_custom_call" | custom-call | tf_op jit(solution)/shard_map/ptychography/pallas_call | solution.py:443
  86.8 0.0 copy-start
  86.8 2.3 %copy.15 = f32[2,2,256,256]{3,2,1,0:T(8,128)} copy(f32[2,2,256,256]{3,2,1,0:T(8,128)} %get-tuple-element.4) | data formatting | bytes 2097152
  89.2 0.0 copy-done
  89.2 0.8 copy.16
Async XLA Ops:
  1.3 0.7 copy-start.1
  86.8 2.4 %copy-start = (f32[2,256,256]{2,1,0:T(8,128)S(1)}, f32[2,256,256]{2,1,0:T(8,128)}, u32[]{:S(2)}) copy-start(f32[2,256,256]{2,1,0:T(8,128)} %get-tuple-element.5) | copy-start | bytes 1572868

commit v2 on v1

v2 whole, which is shorter than its diff:
```python
import functools
import math

import jax
import jax.numpy as jnp
import ml_dtypes
import numpy as np
from jax import lax
from jax.experimental import pallas as pl
from jax.experimental.pallas import tpu as pltpu
from jax.sharding import PartitionSpec as P

F32, BF16 = jnp.float32, jnp.bfloat16
MESH = pl.DeviceIdType.MESH
EVEN, EVEN_T, ODD, ODD_T = 0, 2, 4, 6
CHUNK = 32


def split_table(table):
    high = table.astype(ml_dtypes.bfloat16)
    return [high, (table - high.astype(np.float64)).astype(ml_dtypes.bfloat16)]


def dft_tables(width):
    half = width // 2
    out = []
    for parity in range(2):
        k = np.arange(half)[:, None] * 2 + parity
        n = np.arange(half)[None, :]
        angle = 2.0 * math.pi * ((k * n) % width) / width
        c, s = np.cos(angle) / math.sqrt(width), np.sin(angle) / math.sqrt(width)
        block = np.block([[c, s], [-s, c]])
        out += split_table(block) + split_table(block.T)
    return np.stack(out)


def order_tables(width):
    half = width // 2
    order = np.concatenate([np.arange(half) * 2, np.arange(half) * 2 + 1])
    perm = np.zeros((width, width))
    perm[order, np.arange(width)] = 1.0
    return np.stack([perm, perm.T]).astype(ml_dtypes.bfloat16)


def cat(parts, axis):
    return jnp.concatenate(parts, axis=axis)


def split(x):
    high = x.astype(BF16)
    return high, (x - high.astype(F32)).astype(BF16)


def mm(a, b):
    return jnp.dot(a, b, preferred_element_type=F32)


def right(x, tables, at):
    high, low = split(x)
    th, tl = tables[at], tables[at + 1]
    return mm(high, th) + mm(low, th) + mm(high, tl)


def left(tables, at, x):
    high, low = split(x)
    th, tl = tables[at], tables[at + 1]
    return mm(th, high) + mm(th, low) + mm(tl, high)


def forward(fields, tables):
    h = fields[0][0].shape[1] // 2
    mid, out = [], []
    for re, im in fields:
        u = cat([re[:, :h] + re[:, h:], im[:, :h] + im[:, h:]], 1)
        v = cat([re[:, :h] - re[:, h:], im[:, :h] - im[:, h:]], 1)
        mid.append((right(u, tables, EVEN_T), right(v, tables, ODD_T)))
    for e, o in mid:
        es, os = e[:h] + e[h:], o[:h] + o[h:]
        ed, od = e[:h] - e[h:], o[:h] - o[h:]
        a = cat([cat([es[:, :h], os[:, :h]], 1), cat([es[:, h:], os[:, h:]], 1)], 0)
        b = cat([cat([ed[:, :h], od[:, :h]], 1), cat([ed[:, h:], od[:, h:]], 1)], 0)
        out.append((left(tables, EVEN, a), left(tables, ODD, b)))
    return out


def inverse(fields, tables):
    h = fields[0][0].shape[0] // 2
    mid, out = [], []
    for a, b in fields:
        mid.append((left(tables, EVEN_T, a), left(tables, ODD_T, b)))
    for e, o in mid:
        t, w = e + o, e - o
        qe = cat([cat([t[:h, :h], t[h:, :h]], 1), cat([w[:h, :h], w[h:, :h]], 1)], 0)
        qo = cat([cat([t[:h, h:], t[h:, h:]], 1), cat([w[:h, h:], w[h:, h:]], 1)], 0)
        e, o = right(qe, tables, EVEN), right(qo, tables, ODD)
        s, d = e + o, e - o
        out.append((cat([s[:, :h], d[:, :h]], 1), cat([s[:, h:], d[:, h:]], 1)))
    return out


def freq_mul(a, k, conj):
    h = a.shape[0] // 2
    kr, ki, ar, ai = k[:h], k[h:], a[:h], a[h:]
    if conj:
        return cat([kr * ar + ki * ai, kr * ai - ki * ar], 0)
    return cat([kr * ar - ki * ai, kr * ai + ki * ar], 0)


def reorder(x, order):
    high, low = split(x)
    high, low = split(mm(high, order[0]) + mm(low, order[0]))
    return mm(order[1], high) + mm(order[1], low)


def turn(x, down, along):
    return pltpu.roll(pltpu.roll(x, along, 1), down, 0)


def kernel(
    W, NR, NC,
    obj, probe_in, prop_in, meas_in, pos, cnt, tables_in, order_in,
    grad_out, probe_out,
    ext, gext, probe, prop, meas, tables, order, kperm, mperm, probes, patches, waves, grads, psum,
    rbuf, cbuf, swapped, landed, zbuf, piece_all, other, level_in,
    load_sem, halo_send, halo_recv, grow_send, grow_recv, gcol_send, gcol_recv,
    swap_sem, rs_send, rs_recv, rz_send, rz_recv, ac_send, ac_recv, lv_send, lv_recv,
):
    h = W // 2
    far = h + W
    cap = meas.shape[0]
    zs = NR // 2
    piece_rows = 2 * W // NC
    row, col = lax.axis_index("row"), lax.axis_index("col")
    core, z = lax.rem(row, 2), lax.div(row, 2)
    twin = (row + 1 - 2 * core, col)
    to_left, to_right = (row, lax.rem(col + NC - 1, NC)), (row, lax.rem(col + 1, NC))

    halves = [core, 1 - core]
    row_peers = [(lax.rem(row + NR + 2 * q - 1, NR), col) for q in halves]

    def span(start):
        return pl.ds(pl.multiple_of(start, h), h)

    def remote(src, dst, send, recv, device):
        return pltpu.make_async_remote_copy(
            src_ref=src, dst_ref=dst, send_sem=send, recv_sem=recv,
            device_id=device, device_id_type=MESH,
        )

    barrier = pltpu.get_barrier_semaphore()

    def greet(device):
        pl.semaphore_signal(barrier, inc=1, device_id=device, device_id_type=MESH)

    def greet_col(d, carry):
        greet((row, lax.rem(col + d, NC)))
        return carry

    def greet_row(d, carry):
        greet((lax.rem(row + 2 * d, NR), col))
        return carry

    for device in row_peers:
        greet(device)
    lax.fori_loop(1, NC, greet_col, 0)
    lax.fori_loop(1, zs, greet_row, 0)
    loads = [
        pltpu.make_async_copy(src, dst, load_sem.at[n])
        for n, (src, dst) in enumerate((
            (prop_in, prop), (order_in, order), (probe_in, probe), (meas_in, meas), (tables_in, tables),
            (obj, ext.at[:, :, h:far, h:far]),
        ))
    ]
    for c in loads:
        c.start()
    pl.semaphore_wait(barrier, NC + zs)

    halos = []
    for s in range(2):
        sides, middles, corners = [], [], []
        for t, q in enumerate(halves):
            for side in range(2):
                n = s * 10 + t * 2 + side
                lanes = pl.ds(0, h) if side == 0 else pl.ds(far, h)
                sides.append(remote(
                    obj.at[s, :, span(q * h), pl.ds(h, h) if side == 0 else pl.ds(0, h)],
                    ext.at[s, :, span(h + q * h), lanes],
                    halo_send.at[n], halo_recv.at[n], to_right if side == 0 else to_left,
                ))
                corners.append(remote(
                    ext.at[s, :, span(h + q * h), lanes],
                    ext.at[s, :, span((1 - q) * far), lanes],
                    halo_send.at[n + 4], halo_recv.at[n + 4], row_peers[t],
                ))
            n = s * 10 + 8 + t
            middles.append(remote(
                obj.at[s, :, span(q * h), :],
                ext.at[s, :, span((1 - q) * far), pl.ds(h, W)],
                halo_send.at[n], halo_recv.at[n], row_peers[t],
            ))
        halos.append((sides, middles, corners))
    for sides, middles, corners in halos:
        for c in sides + middles:
            c.start()

    def forward_corners(s):
        sides, middles, corners = halos[s]
        for side, corner in zip(sides, corners):
            side.wait_recv()
            corner.start()

    def finish_halo(s):
        sides, middles, corners = halos[s]
        for c in middles + corners:
            c.wait_recv()

    rows = lax.broadcasted_iota(jnp.int32, (W, W), 0)
    cols = lax.broadcasted_iota(jnp.int32, (W, W), 1)
    count = cnt[0]

    def start_of(k):
        return jnp.clip(pos[0, k] + h, 0, W), jnp.clip(pos[1, k] + h, 0, W)

    def prepare(k, total):
        r0, c0 = start_of(k)
        m = meas[k]
        mperm[k] = reorder(m, order)
        probes[k, 0] = turn(probe[0], lax.rem(r0, W), lax.rem(c0, W))
        probes[k, 1] = turn(probe[1], lax.rem(r0, W), lax.rem(c0, W))
        return total + jnp.where(k < count, jnp.sum(m.reshape(W // 8, 8, W), axis=0), 0.0)

    def pick(k, s, ri):
        r0, c0 = start_of(k)
        inr, inc = rows < r0, cols < c0
        q = [[ext[s, ri, a * W:(a + 1) * W, b * W:(b + 1) * W] for b in range(2)] for a in range(2)]
        return jnp.where(inr, jnp.where(inc, q[1][1], q[1][0]), jnp.where(inc, q[0][1], q[0][0]))

    def pair(i):
        return [2 * i, 2 * i + 1]

    def phase_a(i, carry):
        exits = []
        for k in pair(i):
            pr, pi = probes[k, 0], probes[k, 1]
            ore, oim = pick(k, 0, 0), pick(k, 0, 1)
            patches[k, 0] = ore
            patches[k, 1] = oim
            exits.append((pr * ore - pi * oim, pr * oim + pi * ore))
        far_fields = forward(exits, tables)
        far_fields = [
            (freq_mul(a, kperm[0], False), freq_mul(b, kperm[1], False)) for a, b in far_fields
        ]
        for k, (wr, wi) in zip(pair(i), inverse(far_fields, tables)):
            waves[k, 0] = wr
            waves[k, 1] = wi
        return carry

    def phase_b(i, carry):
        exits, objects = [], []
        for k in pair(i):
            wr, wi = waves[k, 0], waves[k, 1]
            ore, oim = pick(k, 1, 0), pick(k, 1, 1)
            objects.append((ore, oim))
            exits.append((wr * ore - wi * oim, wr * oim + wi * ore))
        scaled = []
        for k, (a, b) in zip(pair(i), forward(exits, tables)):
            fa = a[:h] * a[:h] + a[h:] * a[h:] - mperm[k, :h, :]
            fb = b[:h] * b[:h] + b[h:] * b[h:] - mperm[k, h:, :]
            scaled.append((cat([fa * a[:h], fa * a[h:]], 0), cat([fb * b[:h], fb * b[h:]], 0)))
        for k, (ore, oim), (gr, gi) in zip(pair(i), objects, inverse(scaled, tables)):
            wr, wi = waves[k, 0], waves[k, 1]
            grads[k, 0] = jnp.where(k < count, wr * gr + wi * gi, 0.0)
            grads[k, 1] = jnp.where(k < count, wr * gi - wi * gr, 0.0)
            waves[k, 0] = ore * gr + oim * gi
            waves[k, 1] = ore * gi - oim * gr
        return carry

    def phase_c(i, carry):
        far_fields = forward([(waves[k, 0], waves[k, 1]) for k in pair(i)], tables)
        far_fields = [
            (freq_mul(a, kperm[0], True), freq_mul(b, kperm[1], True)) for a, b in far_fields
        ]
        for k, (gr, gi) in zip(pair(i), inverse(far_fields, tables)):
            used = k < count
            r0, c0 = start_of(k)
            pr, pi = probes[k, 0], probes[k, 1]
            grads[k, 0] = jnp.where(used, pr * gr + pi * gi, 0.0)
            grads[k, 1] = jnp.where(used, pr * gi - pi * gr, 0.0)
            ore, oim = patches[k, 0], patches[k, 1]
            for n, x in enumerate((ore * gr + oim * gi, ore * gi - oim * gr)):
                x = turn(jnp.where(used, x, 0.0), lax.rem(W - r0, W), lax.rem(W - c0, W))
                psum[n, :W, :] += x[:, :h]
                psum[n, W:2 * W, :] += x[:, h:]
        return carry

    def place(s):
        chunk_rows = lax.broadcasted_iota(jnp.int32, (CHUNK, W), 0)
        chunk_cols = lax.broadcasted_iota(jnp.int32, (CHUNK, W), 1)

        def one(at, carry):
            base = pl.multiple_of(at * CHUNK, CHUNK)
            starts = [start_of(k) for k in range(cap)]
            inr = [chunk_rows < r0 - base for r0, c0 in starts]
            inc = [chunk_cols < c0 for r0, c0 in starts]
            for ri in range(2):
                g = [grads[k, ri, pl.ds(base, CHUNK), :] for k in range(cap)]
                high = [jnp.where(inr[k], g[k], 0.0) for k in range(cap)]
                for qa in range(2):
                    part = high if qa else [g[k] - high[k] for k in range(cap)]
                    far_side = [jnp.where(inc[k], part[k], 0.0) for k in range(cap)]
                    near_side = [part[k] - far_side[k] for k in range(cap)]
                    at_rows = pl.ds(pl.multiple_of(qa * W + base, CHUNK), CHUNK)
                    gext[s, ri, at_rows, pl.ds(0, W)] = sum(near_side[1:], near_side[0])
                    gext[s, ri, at_rows, pl.ds(W, W)] = sum(far_side[1:], far_side[0])
            return carry

        lax.fori_loop(0, W // CHUNK, one, 0)

    def share_levels(d):
        return remote(level_in.at[col], level_in.at[col], lv_send.at[d], lv_recv.at[d], (row, lax.rem(col + d, NC)))

    row_copies, col_copies = [], []
    for s in range(2):
        edges, centres, sides = [], [], []
        for t, q in enumerate(halves):
            for at, (first, size) in enumerate(((0, h), (far, h), (h, W))):
                n = s * 6 + t * 3 + at
                (centres if at == 2 else edges).append(remote(
                    gext.at[s, :, span(q * far), pl.ds(first, size)],
                    rbuf.at[s, t, :, :, pl.ds(first, size)],
                    grow_send.at[n], grow_recv.at[n], row_peers[t],
                ))
            for side in range(2):
                n = s * 4 + t * 2 + side
                sides.append(remote(
                    gext.at[s, :, span(h + q * h), pl.ds(0, h) if side == 0 else pl.ds(far, h)],
                    cbuf.at[s, t, side],
                    gcol_send.at[n], gcol_recv.at[n], to_left if side == 0 else to_right,
                ))
        row_copies.append((edges, centres))
        col_copies.append(sides)

    def send_rows(s):
        for c in row_copies[s][0] + row_copies[s][1]:
            c.start()

    def send_cols(s):
        for t, q in enumerate(halves):
            for side in range(2):
                lanes = pl.ds(0, h) if side == 0 else pl.ds(far, h)
                row_copies[s][0][t * 2 + side].wait_recv()
                for ri in range(2):
                    gext[s, ri, span(h + q * h), lanes] += rbuf[s, t, ri, :, lanes]
                col_copies[s][t * 2 + side].start()

    def finish_grad(s, mean):
        for t, q in enumerate(halves):
            row_copies[s][1][t].wait_recv()
            for side in range(2):
                col_copies[s][t * 2 + side].wait_recv()
                c = 1 - side
                lanes = pl.ds(h + c * h, h)
                for ri in range(2):
                    grad_out[s, ri, span(q * h), c * h:(c + 1) * h] = (
                        gext[s, ri, span(h + q * h), lanes]
                        + rbuf[s, t, ri, :, lanes]
                        + cbuf[s, t, side, ri]
                    ) / mean

    def split_planes():
        return remote(psum.at[1 - core], swapped, swap_sem.at[0], swap_sem.at[1], twin)

    def scatter_col(d):
        peer = lax.rem(col + d, NC)
        src = psum.at[core, pl.ds(pl.multiple_of(peer * piece_rows, piece_rows), piece_rows), :]
        return remote(src, landed.at[col], rs_send.at[d], rs_recv.at[d], (row, peer))

    def share_z(d):
        return remote(zbuf.at[z], zbuf.at[z], rz_send.at[d], rz_recv.at[d], (lax.rem(row + 2 * d, NR), col))

    def gather_col(d):
        return remote(piece_all.at[col], piece_all.at[col], ac_send.at[d], ac_recv.at[d], (row, lax.rem(col + d, NC)))

    def join_planes():
        return remote(piece_all, other, swap_sem.at[2], swap_sem.at[3], twin)

    def run(make, hi, what):
        def step(d, carry):
            getattr(make(d), what)()
            return carry

        lax.fori_loop(1, hi, step, 0)

    psum[...] = jnp.zeros_like(psum)
    for c in loads[:2]:
        c.wait()
    kr, ki = reorder(prop[0], order), reorder(prop[1], order)
    kperm[0] = cat([kr[:h], ki[:h]], 0)
    kperm[1] = cat([kr[h:], ki[h:]], 0)
    for c in loads[2:4]:
        c.wait()
    total = jnp.sum(lax.fori_loop(0, cap, prepare, jnp.zeros((8, W), F32)))
    first_rows = lax.broadcasted_iota(jnp.int32, (8, h), 0) < 4
    level_in[col] = jnp.where(first_rows, total, count.astype(F32))
    run(share_levels, NC, "start")
    for c in loads[4:]:
        c.wait()
    forward_corners(0)
    finish_halo(0)
    lax.fori_loop(0, cap // 4, phase_a, 0)
    forward_corners(1)
    lax.fori_loop(cap // 4, cap // 2, phase_a, 0)
    run(share_levels, NC, "wait_recv")
    got = level_in[0]
    for j in range(1, NC):
        got = got + level_in[j]
    psum[0, 2 * W:, :] = got
    psum[1, 2 * W:, :] = got
    finish_halo(1)
    lax.fori_loop(0, cap // 4, phase_b, 0)
    lax.fori_loop(cap // 4, cap // 2, phase_b, 0)
    place(1)
    send_rows(1)
    lax.fori_loop(0, cap // 4, phase_c, 0)
    lax.fori_loop(cap // 4, cap // 2, phase_c, 0)
    split_planes().start()
    place(0)
    send_rows(0)
    split_planes().wait_recv()
    psum[core] += swapped[...]
    run(scatter_col, NC, "start")
    send_cols(1)
    landed[col] = psum[core, pl.ds(pl.multiple_of(col * piece_rows, piece_rows), piece_rows), :]
    run(scatter_col, NC, "wait_recv")
    got = landed[0]
    for j in range(1, NC):
        got = got + landed[j]
    zbuf[z, :piece_rows, :] = got
    zbuf[z, piece_rows:, :] = psum[core, 2 * W:, :]
    run(share_z, zs, "start")
    send_cols(0)
    run(share_z, zs, "wait_recv")
    got = zbuf[0]
    for j in range(1, zs):
        got = got + zbuf[j]
    scans = got[piece_rows + 4:piece_rows + 5, :1]
    mean = got[piece_rows:piece_rows + 1, :1] / (scans * float(W * W))
    piece_all[col] = got[:piece_rows] / (mean * scans)
    run(gather_col, NC, "start")
    finish_grad(1, mean)
    finish_grad(0, mean)
    run(gather_col, NC, "wait_recv")
    join_planes().start()
    per_half = NC // 2
    for half in range(2):
        for j in range(per_half):
            probe_out[core, j * piece_rows:(j + 1) * piece_rows, half * h:(half + 1) * h] = (
                piece_all[half * per_half + j]
            )
    join_planes().wait_recv()
    for half in range(2):
        for j in range(per_half):
            probe_out[1 - core, j * piece_rows:(j + 1) * piece_rows, half * h:(half + 1) * h] = (
                other[half * per_half + j]
            )
    for sides, middles, corners in halos:
        for c in sides + middles + corners:
            c.wait_send()
    for s in range(2):
        for c in row_copies[s][0] + row_copies[s][1] + col_copies[s]:
            c.wait_send()
    for c in [split_planes(), join_planes()]:
        c.wait_send()
    run(share_levels, NC, "wait_send")
    run(scatter_col, NC, "wait_send")
    run(share_z, zs, "wait_send")
    run(gather_col, NC, "wait_send")


def on_device(NR, NC, object_slices, probe_wave, propagator, measured, positions, scan_counts):
    W = probe_wave.shape[1]
    h = W // 2
    cap = measured.shape[2]
    zs = NR // 2
    piece_rows = 2 * W // NC
    vmem, smem = pl.BlockSpec(memory_space=pltpu.VMEM), pl.BlockSpec(memory_space=pltpu.SMEM)
    anywhere = pl.BlockSpec(memory_space=pl.ANY)
    V, D = pltpu.VMEM, pltpu.SemaphoreType.DMA
    return pl.pallas_call(
        functools.partial(kernel, W, NR, NC),
        out_shape=(
            pltpu.VMEM((2, 2, W, W), F32),
            pltpu.VMEM((2, W, W), F32),
        ),
        in_specs=[anywhere] * 4 + [smem] * 2 + [anywhere] * 2,
        out_specs=(vmem, vmem),
        scratch_shapes=[
            V((2, 2, 2 * W, 2 * W), F32),
            V((2, 2, 2 * W, 2 * W), F32),
            V((2, W, W), F32),
            V((2, W, W), F32),
            V((cap, W, W), F32),
            V((8, W, W), BF16),
            V((2, W, W), BF16),
            V((2, W, W), F32),
            V((cap, W, W), F32),
            V((cap, 2, W, W), F32),
            V((cap, 2, W, W), F32),
            V((cap, 2, W, W), F32),
            V((cap, 2, W, W), F32),
            V((2, 2 * W + 8, h), F32),
            V((2, 2, 2, h, 2 * W), F32),
            V((2, 2, 2, 2, h, h), F32),
            V((2 * W + 8, h), F32),
            V((NC, piece_rows, h), F32),
            V((zs, piece_rows + 8, h), F32),
            V((NC, piece_rows, h), F32),
            V((NC, piece_rows, h), F32),
            V((NC, 8, h), F32),
            D((6,)), D((20,)), D((20,)), D((12,)), D((12,)), D((8,)), D((8,)),
            D((4,)), D((NC,)), D((NC,)), D((zs,)), D((zs,)), D((NC,)), D((NC,)),
            D((NC,)), D((NC,)),
        ],
        compiler_params=pltpu.CompilerParams(
            collective_id=0, has_side_effects=True, vmem_limit_bytes=56 * 1024 * 1024
        ),
        name="ptychography",
    )(
        object_slices, probe_wave, propagator, measured[0, 0], positions[0, 0].T,
        scan_counts[0], jnp.asarray(dft_tables(W)), jnp.asarray(order_tables(W)),
    )


def solution(mesh):
    placed = (
        P(None, None, "row", "col"),
        P(),
        P(),
        P("row", "col", None, None, None),
        P("row", "col", None, None),
        P("row", "col"),
    )
    return jax.shard_map(
        functools.partial(on_device, mesh.shape["row"], mesh.shape["col"]),
        mesh=mesh,
        in_specs=placed,
        out_specs=(P(None, None, "row", "col"), P()),
        check_vma=False,
    )
```

time: 91.1 us -> 70.1 us (0.77); the launches traced: 90 us -> 70 us
  Pallas kernels: 84.2 us -> 67 us
  local copies, waits for them, and re-layouts: 4.5 us -> 1.77 us
    pallas_call x1, Pallas kernels: 84.2 us -> 67 us  [on_device(): pl.pallas_call(functools.partial(kernel, W, NR, NC), out_shape=(pltpu.VME...]
    unnamed x7 -> x2, local copies, waits for them, and re-layouts: 3.9 us -> 1.77 us
where the time goes in v2:
time: 70.1 us; the launch traced here: 70 us
  Pallas kernels  67 us (96%)
  local copies, waits for them, and re-layouts  1.77 us (3%)
  between operations  1.29 us (2%)
    pallas_call x1, Pallas kernels, on_device(): pl.pallas_call(functools.partial(kernel, W, NR, NC), out_shape=(pltpu.VME...  67 us
    unnamed x2, local copies, waits for them, and re-layouts  1.77 us

profile of v2, /device:TPU:1, one launch (start us, length us, event | category | flops | bytes accessed | tf_op | source)
XLA Modules:
  0.0 70.0 jit_solution(4174005340524038069)
XLA Ops:
  1.3 67.0 %ptychography.1 = (f32[2,2,256,256]{3,2,1,0:T(8,128)S(1)}, f32[2,256,256]{2,1,0:T(8,128)S(1)}) custom-call(f32[2,2,256,256]{3,2,1,0:T(8,128)} %obj.1, f32[2,256,256]{2,1,0:T(8,128)} %probe_in.1, f32[2,256,256]{2,1,0:T(8,128)} %prop_in.1, f32[4,256,256]{2,1,0:T(8,128)} %bitcast.6, s32[2,4]{1,0:T(2,128)} %bitcast.7, s32[1]{0:T(128)} %bitcast.5.cnt, ...), custom_call_target="tpu_custom_call" | custom-call | tf_op jit(solution)/shard_map/ptychography/pallas_call | solution.py:489
  68.3 1.0 %copy.12 = f32[2,2,256,256]{3,2,1,0:T(8,128)} copy(f32[2,2,256,256]{3,2,1,0:T(8,128)S(1)} %get-tuple-element.2) | data formatting | bytes 2097152
  69.2 0.8 %copy.13 = f32[2,256,256]{2,1,0:T(8,128)} copy(f32[2,256,256]{2,1,0:T(8,128)S(1)} %get-tuple-element.3) | data formatting | bytes 1048576

commit v3 on v2

--- a/solution.py
+++ b/solution.py
@@ -424,12 +424,12 @@
     lax.fori_loop(0, cap // 4, phase_c, 0)
     lax.fori_loop(cap // 4, cap // 2, phase_c, 0)
     split_planes().start()
-    place(0)
-    send_rows(0)
     split_planes().wait_recv()
     psum[core] += swapped[...]
     run(scatter_col, NC, "start")
     send_cols(1)
+    place(0)
+    send_rows(0)
     landed[col] = psum[core, pl.ds(pl.multiple_of(col * piece_rows, piece_rows), piece_rows), :]
     run(scatter_col, NC, "wait_recv")
     got = landed[0]

time: 70.1 us -> 69.2 us (0.987)
  Pallas kernels: 67 us -> 66.1 us
    pallas_call x1, Pallas kernels: 67 us -> 66.1 us  [on_device(): pl.pallas_call(functools.partial(kernel, W, NR, NC), out_shape=(pltpu.VME...]
where the time goes in v3:
time: 69.2 us; the launch traced here: 69.1 us
  Pallas kernels  66.1 us (96%)
  local copies, waits for them, and re-layouts  1.77 us (3%)
  between operations  1.29 us (2%)
    pallas_call x1, Pallas kernels, on_device(): pl.pallas_call(functools.partial(kernel, W, NR, NC), out_shape=(pltpu.VME...  66.1 us
    unnamed x2, local copies, waits for them, and re-layouts  1.77 us

profile of v3, /device:TPU:1, one launch (start us, length us, event | category | flops | bytes accessed | tf_op | source)
XLA Modules:
  0.0 69.1 jit_solution(8263072169682199915)
XLA Ops:
  1.3 66.1 %ptychography.1 = (f32[2,2,256,256]{3,2,1,0:T(8,128)S(1)}, f32[2,256,256]{2,1,0:T(8,128)S(1)}) custom-call(f32[2,2,256,256]{3,2,1,0:T(8,128)} %obj.1, f32[2,256,256]{2,1,0:T(8,128)} %probe_in.1, f32[2,256,256]{2,1,0:T(8,128)} %prop_in.1, f32[4,256,256]{2,1,0:T(8,128)} %bitcast.6, s32[2,4]{1,0:T(2,128)} %bitcast.7, s32[1]{0:T(128)} %bitcast.5.cnt, ...), custom_call_target="tpu_custom_call" | custom-call | tf_op jit(solution)/shard_map/ptychography/pallas_call | solution.py:489
  67.4 1.0 %copy.12 = f32[2,2,256,256]{3,2,1,0:T(8,128)} copy(f32[2,2,256,256]{3,2,1,0:T(8,128)S(1)} %get-tuple-element.2) | data formatting | bytes 2097152
  68.3 0.8 %copy.13 = f32[2,256,256]{2,1,0:T(8,128)} copy(f32[2,256,256]{2,1,0:T(8,128)S(1)} %get-tuple-element.3) | data formatting | bytes 1048576
